TPU v7x, 32 devices: a whole 2x2x4 slice. The times are simulated.
32 devices in a mesh: front: 8 (over z, core), tile: 4 (over y, x).
Axes of the slice: x: 2, y: 2, z: 4, core: 2. Of those that a mesh axis runs over, the one named last changes fastest.
Arguments:
- pieces: bfloat16 [2304, 256, 128], P(('front', 'tile')), may hold values from -1.59375 to 1.59375
- dest_front: int32 [2304, 1], P(('front', 'tile')), may hold values from 0 to 7; in each aligned block of 72 rows (0 to 71, 72 to 143, ...) at most 9 rows name the same one
- dest_slot: int32 [2304], P(('front', 'tile')), may hold values from 0 to 3
- parent_u: bfloat16 [2048, 1024], P('front', 'tile'), may hold values from -1.59375 to 1.59375
- parent_v: bfloat16 [2048, 1024], P('front', 'tile'), may hold values from -1.59375 to 1.59375
- sketch: bfloat16 [256, 64], replicated, may hold values from -6 to 6
- pivot_inverse: bfloat16 [2048, 256], P('front'), may hold values from -0.01171875 to 0.01171875
Outputs:
- coeff: bfloat16 [2048, 1024], P('front', 'tile')
- cores: float32 [8192, 1024], P(('front', 'tile'))
Inputs may be any that keep to these rules, and one draw needn't show every extreme that they name: `dest_front`: among the 72 rows of one device at most 9 name any one front, a bound that some block reaches.
All inputs are finite; a program needn't handle non-finite values.
Results may differ from a plain program's by a relative error of at most 0.017.
Values may be sent and summed in bfloat16 or wider, within the bound.
A program may use at most 128 MiB of HBM per device.

v0:
```python
import jax
import jax.numpy as jnp
from jax import lax
from jax.sharding import PartitionSpec as P

B = 256
R = 64
TILES_DEV = 4
CAP = 9


def sketch_pass(arrived, sketch):
    left_rows = arrived[..., :R]
    right_rows = arrived[..., R:]
    small = jnp.einsum(
        "...br,bk->...rk", right_rows, sketch, preferred_element_type=jnp.float32
    ).astype(jnp.bfloat16)
    return jnp.einsum("...br,...rk->...bk", left_rows, small, preferred_element_type=jnp.float32)


def orthonormal_basis(block_unit):
    gram_matrix = jnp.einsum(
        "naj,nav->njv", block_unit, block_unit, precision=lax.Precision.HIGHEST
    )
    lower = jnp.linalg.cholesky(gram_matrix)
    solved = jax.scipy.linalg.solve_triangular(lower, jnp.swapaxes(block_unit, 1, 2), lower=True)
    return jnp.swapaxes(solved, 1, 2)


def expand(factor, small):
    return jnp.einsum("pbr,prk->pbk", factor, small, preferred_element_type=jnp.float32)


def project(factor, other):
    return jnp.einsum("pbr,pbk->prk", factor, other, preferred_element_type=jnp.float32).astype(
        jnp.bfloat16
    )


def shards(pieces, dest_front, dest_slot, parent_u, parent_v, sketch, pivot_inverse):
    fronts = lax.axis_size("front")
    front_ids = dest_front[:, 0]
    front_marks = (front_ids[:, None] == jnp.arange(fronts, dtype=jnp.int32)[None, :]).astype(
        jnp.int32
    )
    prior_level = jnp.sum((jnp.cumsum(front_marks, axis=0) - front_marks) * front_marks, axis=1)
    places = front_ids * CAP + prior_level
    outgoing = (
        jnp.zeros((fronts * CAP, B, 2 * R), jnp.bfloat16)
        .at[places]
        .set(pieces)
        .reshape(fronts, CAP, B, 2 * R)
    )
    out_slots = (
        jnp.full((fronts * CAP,), TILES_DEV, jnp.int32)
        .at[places]
        .set(dest_slot)
        .reshape(fronts, CAP)
    )
    received, slot_ids = (
        lax.all_to_all(outgoing, "front", split_axis=0, concat_axis=0, tiled=True),
        lax.all_to_all(out_slots, "front", split_axis=0, concat_axis=0, tiled=True),
    )
    sketched = sketch_pass(received, sketch)
    slot_count = fronts * CAP
    piece_left = received[..., :R].reshape(slot_count, B, R)
    piece_right = received[..., R:].reshape(slot_count, B, R)
    sketched = sketched.reshape(slot_count, B, R)
    owner_mask = (
        slot_ids.reshape(slot_count)[None, :] == jnp.arange(TILES_DEV, dtype=jnp.int32)[:, None]
    )
    owner_float = owner_mask.astype(jnp.float32)
    owner_halves = owner_mask.astype(jnp.bfloat16)
    owned_left_rows = parent_u.reshape(B, TILES_DEV, R).transpose(1, 0, 2)
    own_right = parent_v.reshape(B, TILES_DEV, R).transpose(1, 0, 2)

    def collect(per_piece, parent_term):
        return (
            jnp.einsum("sp,pbk->sbk", owner_float, per_piece, precision=lax.Precision.HIGHEST)
            + parent_term
        )

    def select(field_values):
        return jnp.einsum(
            "eo,elj->olj", owner_halves, field_values, preferred_element_type=jnp.float32
        ).astype(jnp.bfloat16)

    y_start = collect(
        sketched, sketch_pass(jnp.concatenate((owned_left_rows, own_right), axis=2), sketch)
    )
    q_start = orthonormal_basis(y_start).astype(jnp.bfloat16)
    z_mid = collect(
        expand(piece_right, project(piece_left, select(q_start))),
        expand(own_right, project(owned_left_rows, q_start)),
    ).astype(jnp.bfloat16)
    y_end = collect(
        expand(piece_left, project(piece_right, select(z_mid))),
        expand(owned_left_rows, project(own_right, z_mid)),
    )
    q_end = orthonormal_basis(y_end).astype(jnp.bfloat16)
    w_end = collect(
        expand(piece_right, project(piece_left, select(q_end))),
        expand(own_right, project(owned_left_rows, q_end)),
    ).astype(jnp.bfloat16)
    coeff = w_end.transpose(1, 0, 2).reshape(B, TILES_DEV * R)
    pivoted = jnp.dot(pivot_inverse, coeff, preferred_element_type=jnp.float32).astype(jnp.bfloat16)
    cores = jnp.einsum(
        "bi,bj->ij",
        coeff,
        lax.all_gather(pivoted, "tile", axis=1, tiled=True),
        preferred_element_type=jnp.float32,
    )
    return (coeff, cores)


def solution(mesh):
    return jax.shard_map(
        shards,
        mesh=mesh,
        in_specs=(
            P(("front", "tile"), None, None),
            P(("front", "tile"), None),
            P(("front", "tile")),
            P("front", "tile"),
            P("front", "tile"),
            P(),
            P("front", None),
        ),
        out_specs=(P("front", "tile"), P(("front", "tile"), None)),
        check_vma=False,
    )
```

profile of v0, /device:TPU:0, one launch (start us, length us, event | category | flops | bytes accessed | tf_op | source)
XLA Modules:
  0.0 312.9 jit_solution(8563813695101745725)
XLA Ops:
  4.6 6.3 %all-to-all-start = ((s32[8,1,9]{2,1,0:T(1,128)}), s32[8,1,9]{2,1,0:T(1,128)S(1)}, u32[]{:S(2)}, u32[]{:S(2)}) async-start(s32[8,1,9]{2,1,0:T(1,128)} %bitcast.3), calls=%async_computation | async-start | bytes 8192 | tf_op jit(solution)/shard_map/all_to_all | solution.py:62
  11.0 3.3 %broadcast_in_dim.7 = bf16[72,256,128]{2,1,0:T(8,128)(2,1)} broadcast(bf16[]{:T(256)} %constant.46.clone.1), dimensions={} | broadcast | bytes 4718594 | tf_op jit(solution)/shard_map/broadcast_in_dim | solution.py:49
  14.2 14.5 %scatter_fusion = bf16[72,256,128]{2,1,0:T(8,128)(2,1)} fusion(bf16[72,256,128]{2,1,0:T(8,128)(2,1)} %broadcast_in_dim.7, s32[72]{0:T(128)S(1)} %fusion.73, bf16[72,256,128]{2,1,0:T(8,128)(2,1)} %param.10), kind=kCustom, calls=%fused_computation.1 | custom fusion | bytes 14156064 | tf_op jit(solution)/shard_map/scatter | solution.py:51
  28.7 6.7 %copy.125 = bf16[72,256,128]{1,2,0:T(8,128)(2,1)} copy(bf16[72,256,128]{2,1,0:T(8,128)(2,1)} %scatter_fusion) | data formatting | bytes 9437184 | tf_op jit(solution)/shard_map/scatter | solution.py:51
  35.5 5.3 %all-to-all-start.1 = ((bf16[8,9,256,128]{2,3,1,0:T(8,128)(2,1)}), bf16[8,9,256,128]{2,3,1,0:T(8,128)(2,1)}, u32[]{:S(2)}, u32[]{:S(2)}) async-start(bf16[8,9,256,128]{2,3,1,0:T(8,128)(2,1)} %bitcast.111), calls=%async_computation.1 | async-start | bytes 9437184 | tf_op jit(solution)/shard_map/all_to_all | solution.py:61
  42.7 103.4 %all-to-all-done.1 = bf16[8,9,256,128]{2,3,1,0:T(8,128)(2,1)} async-done(((bf16[8,9,256,128]{2,3,1,0:T(8,128)(2,1)}), bf16[8,9,256,128]{2,3,1,0:T(8,128)(2,1)}, u32[]{:S(2)}, u32[]{:S(2)}) %all-to-all-start.1) | async-done | bytes 4718624 | tf_op jit(solution)/shard_map/all_to_all | solution.py:61
  146.1 6.1 %fusion.23 = f32[8,9,256,64]{2,3,1,0:T(8,128)} fusion(bf16[256,64]{0,1:T(8,128)(2,1)S(1)} %copy-done.1, bf16[8,9,256,128]{2,3,1,0:T(8,128)(2,1)} %all-to-all-done.1), kind=kOutput, calls=%fused_computation.23 | convolution fusion | flops 302284800 | bytes 9469952 | tf_op jit(solution)/shard_map/...br,...rk->...bk/dot_general | solution.py:18
  152.2 6.5 %bitcast_add_fusion.5 = (f32[4,256,64]{1,0,2:T(4,128)S(1)}, f32[4,256,64]{1,0,2:T(4,128)S(1)}) fusion(f32[4,64,256]{2,1,0:T(8,128)S(1)} %fusion.49, f32[72,256,64]{1,2,0:T(8,128)} %bitcast.112, s32[72]{0:T(128)S(1)} %eq.34), kind=kOutput, calls=%fused_computation.47 | convolution fusion | flops 56688928 | bytes 5505312 | tf_op jit(solution)/shard_map/sp,pbk->sbk/dot_general | solution.py:79
  159.2 23.5 %custom-call.8 = f32[4,64,64]{2,1,0:T(8,128)S(1)} custom-call(f32[4,64,64]{2,1,0:T(8,128)S(1)} %fusion.62), custom_call_target="Cholesky" | custom-call | tf_op jit(solution)/shard_map/jit(cholesky)/cholesky | solution.py:25
  182.9 19.8 %custom-call.9 = f32[4,1,64,64]{2,3,1,0:T(8,128)S(1)} custom-call(f32[4,1,64,64]{3,2,1,0:T(8,128)S(1)} %select_bitcast_fusion.1), custom_call_target="InvertDiagBlocksLowerTriangular" | custom-call | tf_op jit(solution)/shard_map/jit(_solve_triangular)/vmap()/triangular_solve | solution.py:26
  203.5 2.3 convolution_convert_fusion.2
  205.8 4.4 %fusion.86 = (bf16[8,9,256,64]{2,3,1,0:T(8,128)(2,1)S(1)}, bf16[8,9,256,64]{2,3,1,0:T(8,128)(2,1)}) fusion(bf16[8,9,256,128]{2,3,1,0:T(8,128)(2,1)} %all-to-all-done.1), kind=kLoop, calls=%fused_computation.85 | loop fusion | bytes 9437184 | tf_op jit(solution)/shard_map/slice | solution.py:66
  210.2 5.9 %fusion.31 = f32[72,256,64]{1,2,0:T(8,128)} fusion(bf16[72,256,64]{1,2,0:T(8,128)(2,1)} %bitcast.108, bf16[72,256,64]{1,2,0:T(8,128)(2,1)S(1)} %bitcast.105, bf16[72,256,64]{1,0,2:T(8,128)(2,1)} %convolution_convert_fusion.2), kind=kOutput, calls=%fused_computation.26 | convolution fusion | flops 302284800 | bytes 11796480 | tf_op jit(solution)/shard_map/pbr,prk->pbk/dot_general | solution.py:31
  216.1 6.5 %fusion.45 = bf16[4,256,64]{1,0,2:T(4,128)(2,1)S(1)} fusion(f32[72,256,64]{1,2,0:T(8,128)} %fusion.31, f32[4,64,256]{2,1,0:T(8,128)S(1)} %fusion.50, s32[72]{0:T(128)S(1)} %eq.34), kind=kOutput, calls=%fused_computation.34 | convolution fusion | flops 56754464 | bytes 5112096 | tf_op jit(solution)/shard_map/sp,pbk->sbk/dot_general | solution.py:79
  222.5 2.3 convolution_convert_fusion.1
  225.1 5.9 %fusion.28 = f32[72,256,64]{1,2,0:T(8,128)} fusion(bf16[72,256,64]{1,2,0:T(8,128)(2,1)S(1)} %bitcast.106, bf16[72,256,64]{1,2,0:T(8,128)(2,1)} %bitcast.109, bf16[72,256,64]{1,0,2:T(8,128)(2,1)} %convolution_convert_fusion.1), kind=kOutput, calls=%fused_computation.25 | convolution fusion | flops 302284800 | bytes 11796480 | tf_op jit(solution)/shard_map/pbr,prk->pbk/dot_general | solution.py:31
  231.0 6.7 %bitcast_add_fusion.2 = (f32[4,256,64]{1,0,2:T(4,128)S(1)}, f32[4,256,64]{1,0,2:T(4,128)S(1)}) fusion(f32[4,64,256]{2,1,0:T(8,128)S(1)} %fusion.51, f32[72,256,64]{1,2,0:T(8,128)} %fusion.28, s32[72]{0:T(128)S(1)} %eq.34), kind=kOutput, calls=%fused_computation.45 | convolution fusion | flops 56688928 | bytes 5505312 | tf_op jit(solution)/shard_map/sp,pbk->sbk/dot_general | solution.py:79
  238.9 24.2 %custom-call.10 = f32[4,64,64]{2,1,0:T(8,128)S(1)} custom-call(f32[4,64,64]{2,1,0:T(8,128)} %fusion.60), custom_call_target="Cholesky" | custom-call | tf_op jit(solution)/shard_map/jit(cholesky)/cholesky | solution.py:25
  263.3 20.3 %custom-call.11 = f32[4,1,64,64]{2,3,1,0:T(8,128)} custom-call(f32[4,1,64,64]{3,2,1,0:T(8,128)S(1)} %select_bitcast_fusion), custom_call_target="InvertDiagBlocksLowerTriangular" | custom-call | tf_op jit(solution)/shard_map/jit(_solve_triangular)/vmap()/triangular_solve | solution.py:26
  283.6 1.3 convolution_convert_fusion.4
  285.2 3.0 convolution_convert_fusion
  288.2 5.9 %fusion.25 = f32[72,256,64]{1,2,0:T(8,128)} fusion(bf16[72,256,64]{1,2,0:T(8,128)(2,1)} %bitcast.110, bf16[72,256,64]{1,2,0:T(8,128)(2,1)S(1)} %bitcast.107, bf16[72,256,64]{1,0,2:T(8,128)(2,1)} %convolution_convert_fusion), kind=kOutput, calls=%fused_computation.24 | convolution fusion | flops 302284800 | bytes 11796480 | tf_op jit(solution)/shard_map/pbr,prk->pbk/dot_general | solution.py:31
  294.1 6.5 %fusion.42 = bf16[256,4,64]{0,1,2:T(4,128)(2,1)S(1)} fusion(f32[72,256,64]{1,2,0:T(8,128)} %fusion.25, f32[4,64,256]{2,1,0:T(8,128)S(1)} %fusion.52, s32[72]{0:T(128)S(1)} %copy-done.5), kind=kOutput, calls=%fused_computation.33 | convolution fusion | flops 56754464 | bytes 5112096 | tf_op jit(solution)/shard_map/sp,pbk->sbk/dot_general | solution.py:79
  301.6 10.0 %all_gather.3 = bf16[256,1024]{0,1:T(8,128)(2,1)S(1)} all-gather(bf16[256,256]{0,1:T(8,128)(2,1)S(1)} %fusion.48), channel_id=1, replica_groups=mesh['front'=8,'tile'=4] {'tile'}, dimensions={1}, use_global_device_ids=true | all-gather | bytes 655360 | tf_op jit(solution)/shard_map/all_gather | solution.py:110
  (47 shorter events, 11.6 us)
Async XLA Ops:
  0.6 300.8 %copy-start = (bf16[256,256]{1,0:T(8,128)(2,1)S(1)}, bf16[256,256]{1,0:T(8,128)(2,1)}, u32[]{:S(2)}) copy-start(bf16[256,256]{1,0:T(8,128)(2,1)} %param.16) | copy-start | bytes 393220
  4.6 30.8 %all-to-all-start = ((s32[8,1,9]{2,1,0:T(1,128)}), s32[8,1,9]{2,1,0:T(1,128)S(1)}, u32[]{:S(2)}, u32[]{:S(2)}) async-start(s32[8,1,9]{2,1,0:T(1,128)} %bitcast.3), calls=%async_computation | async-start | bytes 8192 | tf_op jit(solution)/shard_map/all_to_all | solution.py:62
  35.5 5.3 %copy-start.2 = (bf16[256,256]{1,0:T(8,128)(2,1)S(1)}, bf16[256,256]{1,0:T(8,128)(2,1)}, u32[]{:S(2)}) copy-start(bf16[256,256]{1,0:T(8,128)(2,1)} %param.14) | copy-start | bytes 393220
  35.5 5.4 %copy-start.3 = (bf16[256,256]{1,0:T(8,128)(2,1)S(1)}, bf16[256,256]{1,0:T(8,128)(2,1)}, u32[]{:S(2)}) copy-start(bf16[256,256]{1,0:T(8,128)(2,1)} %param.13) | copy-start | bytes 393220
  35.5 5.6 %copy-start.1 = (bf16[256,64]{0,1:T(8,128)(2,1)S(1)}, bf16[256,64]{0,1:T(8,128)(2,1)}, u32[]{:S(2)}) copy-start(bf16[256,64]{0,1:T(8,128)(2,1)} %param.15) | copy-start | bytes 98308
  35.5 110.7 %all-to-all-start.1 = ((bf16[8,9,256,128]{2,3,1,0:T(8,128)(2,1)}), bf16[8,9,256,128]{2,3,1,0:T(8,128)(2,1)}, u32[]{:S(2)}, u32[]{:S(2)}) async-start(bf16[8,9,256,128]{2,3,1,0:T(8,128)(2,1)} %bitcast.111), calls=%async_computation.1 | async-start | bytes 9437184 | tf_op jit(solution)/shard_map/all_to_all | solution.py:61
  42.7 188.3 %copy-start.4 = (s32[72]{0:T(128)}, s32[72]{0:T(128)S(1)}, u32[]{:S(2)}) copy-start(s32[72]{0:T(128)S(1)} %eq.34) | copy-start | bytes 868
  288.2 5.9 %copy-start.5 = (s32[72]{0:T(128)S(1)}, s32[72]{0:T(128)}, u32[]{:S(2)}) copy-start(s32[72]{0:T(128)} %copy-done.4) | copy-start | bytes 868
where the time goes:
time: 314 us; the launch traced here: 313 us
  waiting for transfers between devices  103 us (33%)
  other arithmetic  92 us (29%)
  matrix products  62.7 us (20%)
  local copies, waits for them, and re-layouts  32.3 us (10%)
  starting transfers between devices  11.6 us (4%)
  blocking collectives  10 us (3%)
    all_to_all x1, waiting for transfers between devices, shards(): lax.all_to_all(outgoing, 'front', split_axis=0, concat_axis=0, tiled=True)  103 us
    another operation x7, other arithmetic, orthonormal_basis(): lower = jnp.linalg.cholesky(gram_matrix)  48 us
    another operation x5, other arithmetic, orthonormal_basis(): jax.scipy.linalg.solve_triangular(lower, jnp.swapaxes(block_unit, 1, 2),...  40.3 us
    dot_general x4, matrix products, collect(): jnp.einsum('sp,pbk->sbk', owner_float, per_piece, precision=lax.Precision...  26 us
    scatter x2, local copies, waits for them, and re-layouts, shards(): outgoing = jnp.zeros((fronts * CAP, B, 2 * R), jnp.bfloat16).at[places].s...  21.2 us
    dot_general x6, matrix products, expand(): jnp.einsum('pbr,prk->pbk', factor, small, preferred_element_type=jnp.floa...  18.7 us
    all_gather x1, blocking collectives, shards(): lax.all_gather(pivoted, 'tile', axis=1, tiled=True)  10 us
    dot_general x3, matrix products, select(): jnp.einsum('eo,elj->olj', owner_halves, field_values, preferred_element_t...  7.55 us
  transfers between devices with their start and end apart: 2, of which 1 were waited for; matrix products, arithmetic and copies ran while one was open for 8% of the time, Pallas kernels for 0%

commit v1 on v0

v1 whole, which is shorter than its diff:
```python
import functools

import jax
import jax.numpy as jnp
from jax import lax
from jax.experimental import pallas as pl
from jax.experimental.pallas import tpu as pltpu
from jax.sharding import PartitionSpec as P

B = 256
R = 64
TILES_DEV = 4
CAP = 9
PAIRS = (CAP + 1) // 2
SLOTS = 2 * PAIRS
MESH = pl.DeviceIdType.MESH
F32 = jnp.float32
BF16 = jnp.bfloat16
HIGHEST = lax.Precision.HIGHEST


def dot_nt(a, b, precision=None):
    return lax.dot_general(
        a, b, (((1,), (1,)), ((), ())), precision=precision, preferred_element_type=F32
    )


def dot_nn(a, b, precision=None):
    return lax.dot_general(
        a, b, (((1,), (0,)), ((), ())), precision=precision, preferred_element_type=F32
    )


def merge_kernel(
    chips, table_ref, pieces_ref, pu_ref, pv_ref, out_ref,
    part, ex_out, ex_in, up_out, up_in, dn_out, dn_in,
    ex_send, ex_recv, up_send, up_recv, dn_send, dn_recv,
):
    f = lax.axis_index("front")
    z = lax.div(f, 2)
    c = lax.rem(f, 2)
    sibling = 2 * z + 1 - c
    above = lax.rem(f + 2, 2 * chips)
    below = lax.rem(f + 2 * chips - 2, 2 * chips)
    last = chips - 1

    barrier = pltpu.get_barrier_semaphore()
    pl.semaphore_signal(barrier, inc=1, device_id={"front": sibling}, device_id_type=MESH)

    @pl.when(z > 0)
    def _():
        pl.semaphore_signal(barrier, inc=1, device_id={"front": below}, device_id_type=MESH)

    @pl.when(z < last)
    def _():
        pl.semaphore_signal(barrier, inc=1, device_id={"front": above}, device_id_type=MESH)

    pl.semaphore_wait(barrier, 1 + (z > 0).astype(jnp.int32) + (z < last).astype(jnp.int32))

    def copy(kind, i):
        src, dst, send, recv, peer = {
            "ex": (ex_out, ex_in, ex_send, ex_recv, sibling),
            "up": (up_out, up_in, up_send, up_recv, above),
            "dn": (dn_out, dn_in, dn_send, dn_recv, below),
        }[kind]
        return pltpu.make_async_remote_copy(
            src_ref=src.at[i], dst_ref=dst.at[i], send_sem=send.at[i], recv_sem=recv.at[i],
            device_id={"front": peer}, device_id_type=MESH,
        )

    lane = lax.broadcasted_iota(jnp.int32, (1, 2 * R), 1)

    def partial(e):
        lefts, rights, owners = [], [], []
        for pair in range(PAIRS):
            first = table_ref[e * SLOTS + 2 * pair]
            second = table_ref[e * SLOTS + 2 * pair + 1]
            a = pieces_ref[lax.div(first, 8)]
            b = pieces_ref[lax.div(second, 8)]
            lefts.append(jnp.concatenate((a[:, :R], b[:, :R]), axis=1))
            rights.append(jnp.concatenate((a[:, R:], b[:, R:]), axis=1))
            owners.append(jnp.where(lane < R, lax.rem(first, 8), lax.rem(second, 8)))
        left = jnp.concatenate(lefts, axis=1)
        right = jnp.concatenate(rights, axis=1)
        owner = jnp.concatenate(owners, axis=1)
        sums = []
        for s in range(TILES_DEV):
            mask = jnp.where(owner == s, 1.0, 0.0).astype(BF16)
            sums.append(dot_nt(left * mask, right))
        return sums

    def flow(kind, t, s, incoming):
        i = t * TILES_DEV + s
        copy("ex", i).wait_recv()
        total = part[i] + ex_in[i].astype(F32)
        out = up_out if kind == "up" else dn_out
        if incoming:
            copy(kind, i).wait_recv()
            total = total + (up_in if kind == "up" else dn_in)[i].astype(F32)
        out[i] = total.astype(BF16)
        copy(kind, i).start()

    def end_flows(k):
        @pl.when(z == 0)
        def _():
            lax.fori_loop(0, TILES_DEV, lambda s, _: flow("up", last - k, s, False), None)

        @pl.when(z == last)
        def _():
            lax.fori_loop(0, TILES_DEV, lambda s, _: flow("dn", k, s, False), None)

    def compute(k, _):
        t = jnp.where(2 * z < chips, last - k, k)
        for s, total in enumerate(partial(2 * t + 1 - c)):
            ex_out[t * TILES_DEV + s] = total.astype(BF16)
            copy("ex", t * TILES_DEV + s).start()
        for s, total in enumerate(partial(2 * t + c)):
            part[t * TILES_DEV + s] = total

        @pl.when(k > 0)
        def _():
            end_flows(k - 1)

    lax.fori_loop(0, chips, compute, None)

    for s in range(TILES_DEV):
        cols = slice(s * R, (s + 1) * R)
        part[z * TILES_DEV + s] += dot_nt(pu_ref[:, cols], pv_ref[:, cols])

    def tick(n, _):
        up_n = n - z
        dn_n = n - (last - z)

        @pl.when((up_n >= 0) & (up_n < TILES_DEV * (last - z)))
        def _():
            flow("up", last - lax.div(up_n, TILES_DEV), lax.rem(up_n, TILES_DEV), True)

        @pl.when((dn_n >= 0) & (dn_n < TILES_DEV * z))
        def _():
            flow("dn", lax.div(dn_n, TILES_DEV), lax.rem(dn_n, TILES_DEV), True)

    @pl.when((z > 0) & (z < last))
    def _():
        lax.fori_loop(0, TILES_DEV * last + last, tick, None)

    def finish(s, _):
        i = z * TILES_DEV + s
        copy("ex", i).wait_recv()
        part[i] += ex_in[i].astype(F32)

        @pl.when(z > 0)
        def _():
            copy("up", i).wait_recv()
            part[i] += up_in[i].astype(F32)

        @pl.when(z < last)
        def _():
            copy("dn", i).wait_recv()
            part[i] += dn_in[i].astype(F32)

        out_ref[s] = part[i].astype(BF16)

    lax.fori_loop(0, TILES_DEV, finish, None)

    def drain(i, _):
        copy("ex", i).wait_send()

        @pl.when(i >= TILES_DEV * (z + 1))
        def _():
            copy("up", i).wait_send()

        @pl.when(i < TILES_DEV * z)
        def _():
            copy("dn", i).wait_send()

    lax.fori_loop(0, TILES_DEV * chips, drain, None)


def merge(table, pieces, parent_u, parent_v):
    fronts = lax.axis_size("front")
    chips = fronts // 2
    chunks = chips * TILES_DEV
    tile = (chunks, B, B)
    return pl.pallas_call(
        functools.partial(merge_kernel, chips),
        out_shape=jax.ShapeDtypeStruct((TILES_DEV, B, B), BF16),
        in_specs=[pl.BlockSpec(memory_space=pltpu.SMEM)]
        + [pl.BlockSpec(memory_space=pltpu.VMEM)] * 3,
        out_specs=pl.BlockSpec(memory_space=pltpu.VMEM),
        scratch_shapes=[pltpu.VMEM(tile, F32)]
        + [pltpu.VMEM(tile, BF16)] * 6
        + [pltpu.SemaphoreType.DMA((chunks,))] * 6,
        compiler_params=pltpu.CompilerParams(
            collective_id=0, has_side_effects=True, vmem_limit_bytes=56 * 2**20
        ),
        name="merge",
    )(table, pieces, parent_u, parent_v)


def basis(y, work):
    eye = (
        lax.broadcasted_iota(jnp.int32, (R, R), 0) == lax.broadcasted_iota(jnp.int32, (R, R), 1)
    ).astype(F32)
    for t in range(TILES_DEV):
        gram = dot_nt(y[t], y[t], HIGHEST)
        work[:, t, :] = jnp.concatenate((gram, eye), axis=1)
    rows = [work[i] for i in range(R)]
    for j in range(R):
        row = rows[j]
        pivot = jnp.broadcast_to(row[:, j : j + 1], row.shape)
        scaled = row * (1.0 / pivot)
        for i in range(j + 1, R):
            rows[i] = rows[i] - row[:, i : i + 1] * scaled
        work[j] = row * lax.rsqrt(pivot)
    return [
        dot_nn(work[:, t, :][:, R:], y[t], HIGHEST).astype(BF16) for t in range(TILES_DEV)
    ]


def compress_kernel(m_ref, sketch_ref, pivot_ref, w_ref, coeff_ref, pivoted_ref, work):
    tiles = range(TILES_DEV)
    work[...] = jnp.ones_like(work)
    sketch_t = sketch_ref[...].T
    y = [dot_nt(sketch_t, m_ref[t]) for t in tiles]
    q = basis(y, work)
    mid = [dot_nn(q[t], m_ref[t]).astype(BF16) for t in tiles]
    y = [dot_nt(mid[t], m_ref[t]) for t in tiles]
    q = basis(y, work)
    w = jnp.concatenate([dot_nn(q[t], m_ref[t]) for t in tiles], axis=0)
    w_half = w.astype(BF16)
    w_ref[...] = w_half
    pivoted_ref[...] = dot_nt(w_half, pivot_ref[...]).astype(BF16)
    coeff_ref[...] = w.T.astype(BF16)


def compress(merged, sketch, pivot_inverse):
    wide = TILES_DEV * R
    return pl.pallas_call(
        compress_kernel,
        out_shape=(
            jax.ShapeDtypeStruct((wide, B), BF16),
            jax.ShapeDtypeStruct((B, wide), BF16),
            jax.ShapeDtypeStruct((wide, B), BF16),
        ),
        in_specs=[pl.BlockSpec(memory_space=pltpu.VMEM)] * 3,
        out_specs=[pl.BlockSpec(memory_space=pltpu.VMEM)] * 3,
        scratch_shapes=[pltpu.VMEM((R, 8, 2 * R), F32)],
        compiler_params=pltpu.CompilerParams(vmem_limit_bytes=32 * 2**20),
        name="compress",
    )(merged, sketch, pivot_inverse)


def couple_kernel(ranks, w_ref, p_ref, cores_ref, gathered, send, recv):
    me = lax.axis_index("tile")
    barrier = pltpu.get_barrier_semaphore()
    for d in range(1, ranks):
        peer = lax.rem(me + d, ranks)
        pl.semaphore_signal(barrier, inc=1, device_id={"tile": peer}, device_id_type=MESH)
    pl.semaphore_wait(barrier, ranks - 1)

    def copy(d):
        return pltpu.make_async_remote_copy(
            src_ref=p_ref, dst_ref=gathered.at[d - 1], send_sem=send.at[d - 1],
            recv_sem=recv.at[d - 1], device_id={"tile": lax.rem(me + d, ranks)},
            device_id_type=MESH,
        )

    for d in range(1, ranks):
        copy(d).start()
    wide = TILES_DEV * R

    def place(source, block):
        cores_ref[:, pl.ds(pl.multiple_of(source * wide, wide), wide)] = dot_nt(w_ref[...], block)

    place(me, p_ref[...])
    for d in range(1, ranks):
        copy(d).wait_recv()
        place(lax.rem(me + ranks - d, ranks), gathered[d - 1])
    for d in range(1, ranks):
        copy(d).wait_send()


def couple(w, pivoted):
    ranks = lax.axis_size("tile")
    wide = TILES_DEV * R
    return pl.pallas_call(
        functools.partial(couple_kernel, ranks),
        out_shape=jax.ShapeDtypeStruct((wide, ranks * wide), F32),
        in_specs=[pl.BlockSpec(memory_space=pltpu.VMEM)] * 2,
        out_specs=pl.BlockSpec(memory_space=pltpu.VMEM),
        scratch_shapes=[
            pltpu.VMEM((ranks - 1, wide, B), BF16),
            pltpu.SemaphoreType.DMA((ranks - 1,)),
            pltpu.SemaphoreType.DMA((ranks - 1,)),
        ],
        compiler_params=pltpu.CompilerParams(
            collective_id=1, has_side_effects=True, vmem_limit_bytes=32 * 2**20
        ),
        name="couple",
    )(w, pivoted)


def shards(pieces, dest_front, dest_slot, parent_u, parent_v, sketch, pivot_inverse):
    fronts = lax.axis_size("front")
    count = pieces.shape[0]
    ids = jnp.arange(count, dtype=jnp.int32)
    front_ids = dest_front[:, 0]
    prior = jnp.sum(
        ((front_ids[:, None] == front_ids[None, :]) & (ids[None, :] < ids[:, None])).astype(
            jnp.int32
        ),
        axis=1,
    )
    places = front_ids * SLOTS + prior
    hit = places[:, None] == jnp.arange(fronts * SLOTS, dtype=jnp.int32)[None, :]
    code = (ids * 8 + dest_slot - TILES_DEV)[:, None]
    table = jnp.sum(jnp.where(hit, code, 0), axis=0) + TILES_DEV
    merged = merge(table, pieces, parent_u, parent_v)
    w, coeff, pivoted = compress(merged, sketch, pivot_inverse)
    return (coeff, couple(w, pivoted))


def solution(mesh):
    return jax.shard_map(
        shards,
        mesh=mesh,
        in_specs=(
            P(("front", "tile"), None, None),
            P(("front", "tile"), None),
            P(("front", "tile")),
            P("front", "tile"),
            P("front", "tile"),
            P(),
            P("front", None),
        ),
        out_specs=(P("front", "tile"), P(("front", "tile"), None)),
        check_vma=False,
    )
```

time: 314 us -> 73.3 us (0.23)
  waiting for transfers between devices: 103 us -> 0 us
  other arithmetic: 92 us -> 2.89 us
  Pallas kernels: 0 us -> 65.7 us
  matrix products: 62.7 us -> 0 us
  local copies, waits for them, and re-layouts: 32.3 us -> 2.88 us
  starting transfers between devices: 11.6 us -> 0 us
  blocking collectives: 10 us -> 0 us
    all_to_all x2 -> x0, waiting for transfers between devices: 103 us -> none  [the longest x1 103 us: shards(): lax.all_to_all(outgoing, 'front', split_axis=0, concat_axis=0, tiled=True)]
    another operation x13 -> x0, other arithmetic: 88.4 us -> none  [the longest x7 48 us: orthonormal_basis(): lower = jnp.linalg.cholesky(gram_matrix)]
    pallas_call x0 -> x3, Pallas kernels: none -> 65.7 us  [the longest x1 43.7 us: merge(): pl.pallas_call(functools.partial(merge_kernel, chips), out_shape=jax.Shap...]
    dot_general x19 -> x0, matrix products: 61 us -> none  [the longest x4 26 us: collect(): jnp.einsum('sp,pbk->sbk', owner_float, per_piece, precision=lax.Precision...]
    scatter x3 -> x0, local copies, waits for them, and re-layouts: 22.1 us -> none  [the longest x2 21.2 us: shards(): outgoing = jnp.zeros((fronts * CAP, B, 2 * R), jnp.bfloat16).at[places].s...]
    all_to_all x2 -> x0, starting transfers between devices: 11.6 us -> none  [the longest x1 6.33 us: shards(): lax.all_to_all(out_slots, 'front', split_axis=0, concat_axis=0, tiled=True)]
    all_gather x1 -> x0, blocking collectives: 10 us -> none  [shards(): lax.all_gather(pivoted, 'tile', axis=1, tiled=True)]
    slice x1 -> x0, local copies, waits for them, and re-layouts: 4.39 us -> none  [shards(): piece_left = received[..., :R].reshape(slot_count, B, R)]
  transfers between devices with their start and end apart: 2 -> 0, of which waited for: 1 -> 0; matrix products, arithmetic and copies ran while one was open for 8% -> 0% of each run, Pallas kernels for 0% -> 0%
where the time goes in v1:
time: 73.3 us; the launch traced here: 72.2 us
  Pallas kernels  65.7 us (90%)
  other arithmetic  2.89 us (4%)
  local copies, waits for them, and re-layouts  2.88 us (4%)
    pallas_call x1, Pallas kernels, merge(): pl.pallas_call(functools.partial(merge_kernel, chips), out_shape=jax.Shap...  43.7 us
    pallas_call x1, Pallas kernels, compress(): pl.pallas_call(compress_kernel, out_shape=(jax.ShapeDtypeStruct((wide, B)...  13.4 us
    pallas_call x1, Pallas kernels, couple(): pl.pallas_call(functools.partial(couple_kernel, ranks), out_shape=jax.Sha...  8.68 us
    unnamed x6, local copies, waits for them, and re-layouts  2.88 us

profile of v1, /device:TPU:0, one launch (start us, length us, event | category | flops | bytes accessed | tf_op | source)
XLA Modules:
  0.0 72.2 jit_solution(6439204025835446116)
XLA Ops:
  0.6 0.0 copy-start.1
  0.6 0.7 add_add_fusion
  1.3 0.9 %convert_reduce_fusion = s32[72]{0:T(128)S(1)} fusion(s32[72]{0:T(128)} %bitcast.7), kind=kLoop, calls=%fused_computation.2 | loop fusion | flops 25848 | bytes 576 | tf_op jit(solution)/shard_map/reduce_sum | solution.py:308
  2.2 0.7 fusion.1
  2.9 0.1 select_reduce_fusion
  3.0 0.5 broadcast_add_fusion.table_ref
  3.5 0.9 %copy.10.sketch_ref = bf16[256,64]{1,0:T(8,128)(2,1)S(1)} copy(bf16[256,64]{0,1:T(8,128)(2,1)} %param.12) | data formatting | bytes 65536 | tf_op args[5]
  4.4 43.7 %merge.1.m_ref = bf16[4,256,256]{2,1,0:T(8,128)(2,1)} custom-call(s32[80]{0:T(128)} %broadcast_add_fusion.table_ref, bf16[72,256,128]{2,1,0:T(8,128)(2,1)} %pieces_ref.1, bf16[256,256]{1,0:T(8,128)(2,1)} %pu_ref.1, bf16[256,256]{1,0:T(8,128)(2,1)} %pv_ref.1), custom_call_target="tpu_custom_call" | custom-call | tf_op jit(solution)/shard_map/merge/pallas_call | solution.py:184
  48.1 0.0 copy-done.1
  48.1 0.0 copy-start
  48.1 1.0 %copy-done = bf16[4,256,256]{2,1,0:T(8,128)(2,1)S(1)} copy-done((bf16[4,256,256]{2,1,0:T(8,128)(2,1)S(1)}, bf16[4,256,256]{2,1,0:T(8,128)(2,1)}, u32[]{:S(2)}) %copy-start) | copy-done | bytes 524312
  49.1 13.4 %compress.1 = (bf16[256,256]{1,0:T(8,128)(2,1)S(1)}, bf16[256,256]{1,0:T(8,128)(2,1)}, bf16[256,256]{1,0:T(8,128)(2,1)S(1)}) custom-call(bf16[4,256,256]{2,1,0:T(8,128)(2,1)S(1)} %copy-done, bf16[256,64]{1,0:T(8,128)(2,1)S(1)} %copy.10.sketch_ref, bf16[256,256]{1,0:T(8,128)(2,1)S(1)} %copy-done.1), custom_call_target="tpu_custom_call" | custom-call | tf_op jit(solution)/shard_map/compress/pallas_call | solution.py:238
  62.5 8.7 %couple.1 = f32[256,1024]{1,0:T(8,128)S(1)} custom-call(bf16[256,256]{1,0:T(8,128)(2,1)S(1)} %get-tuple-element.6.w_ref, bf16[256,256]{1,0:T(8,128)(2,1)S(1)} %get-tuple-element.7.p_ref), custom_call_target="tpu_custom_call" | custom-call | tf_op jit(solution)/shard_map/couple/pallas_call | solution.py:286
  71.2 1.0 %copy.12 = f32[256,1024]{1,0:T(8,128)} copy(f32[256,1024]{1,0:T(8,128)S(1)} %couple.1) | data formatting | bytes 2097152
Async XLA Ops:
  0.6 47.4 %copy-start.1 = (bf16[256,256]{1,0:T(8,128)(2,1)S(1)}, bf16[256,256]{1,0:T(8,128)(2,1)}, u32[]{:S(2)}) copy-start(bf16[256,256]{1,0:T(8,128)(2,1)} %pivot_ref.1) | copy-start | bytes 393220
  48.1 1.0 %copy-start = (bf16[4,256,256]{2,1,0:T(8,128)(2,1)S(1)}, bf16[4,256,256]{2,1,0:T(8,128)(2,1)}, u32[]{:S(2)}) copy-start(bf16[4,256,256]{2,1,0:T(8,128)(2,1)} %merge.1.m_ref) | copy-start | bytes 1572868

commit v2 on v1

--- a/solution.py
+++ b/solution.py
@@ -32,7 +32,7 @@
 
 
 def merge_kernel(
-    chips, table_ref, pieces_ref, pu_ref, pv_ref, out_ref,
+    chips, table_ref, pieces_hbm, pu_ref, pv_ref, out_ref, pieces_ref, load_sem,
     part, ex_out, ex_in, up_out, up_in, dn_out, dn_in,
     ex_send, ex_recv, up_send, up_recv, dn_send, dn_recv,
 ):
@@ -44,6 +44,8 @@
     below = lax.rem(f + 2 * chips - 2, 2 * chips)
     last = chips - 1
 
+    load = pltpu.make_async_copy(pieces_hbm, pieces_ref, load_sem)
+    load.start()
     barrier = pltpu.get_barrier_semaphore()
     pl.semaphore_signal(barrier, inc=1, device_id={"front": sibling}, device_id_type=MESH)
 
@@ -56,6 +58,8 @@
         pl.semaphore_signal(barrier, inc=1, device_id={"front": above}, device_id_type=MESH)
 
     pl.semaphore_wait(barrier, 1 + (z > 0).astype(jnp.int32) + (z < last).astype(jnp.int32))
+
+    load.wait()
 
     def copy(kind, i):
         src, dst, send, recv, peer = {
@@ -83,11 +87,9 @@
         left = jnp.concatenate(lefts, axis=1)
         right = jnp.concatenate(rights, axis=1)
         owner = jnp.concatenate(owners, axis=1)
-        sums = []
         for s in range(TILES_DEV):
             mask = jnp.where(owner == s, 1.0, 0.0).astype(BF16)
-            sums.append(dot_nt(left * mask, right))
-        return sums
+            yield dot_nt(left * mask, right)
 
     def flow(kind, t, s, incoming):
         i = t * TILES_DEV + s
@@ -117,9 +119,9 @@
         for s, total in enumerate(partial(2 * t + c)):
             part[t * TILES_DEV + s] = total
 
-        @pl.when(k > 0)
-        def _():
-            end_flows(k - 1)
+        @pl.when(k < last)
+        def _():
+            end_flows(k)
 
     lax.fori_loop(0, chips, compute, None)
 
@@ -184,10 +186,18 @@
     return pl.pallas_call(
         functools.partial(merge_kernel, chips),
         out_shape=jax.ShapeDtypeStruct((TILES_DEV, B, B), BF16),
-        in_specs=[pl.BlockSpec(memory_space=pltpu.SMEM)]
-        + [pl.BlockSpec(memory_space=pltpu.VMEM)] * 3,
+        in_specs=[
+            pl.BlockSpec(memory_space=pltpu.SMEM),
+            pl.BlockSpec(memory_space=pl.ANY),
+            pl.BlockSpec(memory_space=pltpu.VMEM),
+            pl.BlockSpec(memory_space=pltpu.VMEM),
+        ],
         out_specs=pl.BlockSpec(memory_space=pltpu.VMEM),
-        scratch_shapes=[pltpu.VMEM(tile, F32)]
+        scratch_shapes=[
+            pltpu.VMEM(pieces.shape, BF16),
+            pltpu.SemaphoreType.DMA,
+            pltpu.VMEM(tile, F32),
+        ]
         + [pltpu.VMEM(tile, BF16)] * 6
         + [pltpu.SemaphoreType.DMA((chunks,))] * 6,
         compiler_params=pltpu.CompilerParams(
@@ -208,10 +218,11 @@
     for j in range(R):
         row = rows[j]
         pivot = jnp.broadcast_to(row[:, j : j + 1], row.shape)
-        scaled = row * (1.0 / pivot)
+        inverse = lax.rsqrt(pivot)
+        scaled = row * (inverse * inverse)
         for i in range(j + 1, R):
             rows[i] = rows[i] - row[:, i : i + 1] * scaled
-        work[j] = row * lax.rsqrt(pivot)
+        work[j] = row * inverse
     return [
         dot_nn(work[:, t, :][:, R:], y[t], HIGHEST).astype(BF16) for t in range(TILES_DEV)
     ]
@@ -220,7 +231,7 @@
 def compress_kernel(m_ref, sketch_ref, pivot_ref, w_ref, coeff_ref, pivoted_ref, work):
     tiles = range(TILES_DEV)
     work[...] = jnp.ones_like(work)
-    sketch_t = sketch_ref[...].T
+    sketch_t = sketch_ref[...]
     y = [dot_nt(sketch_t, m_ref[t]) for t in tiles]
     q = basis(y, work)
     mid = [dot_nn(q[t], m_ref[t]).astype(BF16) for t in tiles]
@@ -316,7 +327,7 @@
     code = (ids * 8 + dest_slot - TILES_DEV)[:, None]
     table = jnp.sum(jnp.where(hit, code, 0), axis=0) + TILES_DEV
     merged = merge(table, pieces, parent_u, parent_v)
-    w, coeff, pivoted = compress(merged, sketch, pivot_inverse)
+    w, coeff, pivoted = compress(merged, sketch.T, pivot_inverse)
     return (coeff, couple(w, pivoted))
 
 

time: 73.3 us -> 72.5 us (0.989)
  local copies, waits for them, and re-layouts: 2.88 us -> 2.02 us
    pallas_call x1, Pallas kernels: 43.7 us -> 41.7 us  [merge(): pl.pallas_call(functools.partial(merge_kernel, chips), out_shape=jax.Shap...]
    pallas_call x1, Pallas kernels: 8.68 us -> 10.3 us  [couple(): pl.pallas_call(functools.partial(couple_kernel, ranks), out_shape=jax.Sha...]
    unnamed x6 -> x7, local copies, waits for them, and re-layouts: 2.88 us -> 2.02 us
where the time goes in v2:
time: 72.5 us; the launch traced here: 71.4 us
  Pallas kernels  65.8 us (91%)
  other arithmetic  2.89 us (4%)
  local copies, waits for them, and re-layouts  2.02 us (3%)
    pallas_call x1, Pallas kernels, merge(): pl.pallas_call(functools.partial(merge_kernel, chips), out_shape=jax.Shap...  41.7 us
    pallas_call x1, Pallas kernels, compress(): pl.pallas_call(compress_kernel, out_shape=(jax.ShapeDtypeStruct((wide, B)...  13.8 us
    pallas_call x1, Pallas kernels, couple(): pl.pallas_call(functools.partial(couple_kernel, ranks), out_shape=jax.Sha...  10.3 us
    unnamed x7, local copies, waits for them, and re-layouts  2.02 us

profile of v2, /device:TPU:0, one launch (start us, length us, event | category | flops | bytes accessed | tf_op | source)
XLA Modules:
  0.0 71.4 jit_solution(12242057141993423689)
XLA Ops:
  0.6 0.0 copy-start.1
  0.6 0.0 copy-start.2
  0.7 0.7 add_add_fusion
  1.3 0.9 %convert_reduce_fusion = s32[72]{0:T(128)S(1)} fusion(s32[72]{0:T(128)} %bitcast.9), kind=kLoop, calls=%fused_computation.2 | loop fusion | flops 25848 | bytes 576 | tf_op jit(solution)/shard_map/reduce_sum | solution.py:319
  2.3 0.7 fusion.1
  2.9 0.1 select_reduce_fusion
  3.0 0.5 broadcast_add_fusion.table_ref
  3.5 41.7 %merge.1.m_ref = bf16[4,256,256]{2,1,0:T(8,128)(2,1)} custom-call(s32[80]{0:T(128)} %broadcast_add_fusion.table_ref, bf16[72,256,128]{2,1,0:T(8,128)(2,1)} %pieces_hbm.1, bf16[256,256]{1,0:T(8,128)(2,1)} %pu_ref.1, bf16[256,256]{1,0:T(8,128)(2,1)} %pv_ref.1), custom_call_target="tpu_custom_call" | custom-call | tf_op jit(solution)/shard_map/merge/pallas_call | solution.py:186
  45.2 0.0 copy-done.1
  45.3 0.0 copy-done.2
  45.3 0.0 copy-start
  45.3 1.0 %copy-done = bf16[4,256,256]{2,1,0:T(8,128)(2,1)S(1)} copy-done((bf16[4,256,256]{2,1,0:T(8,128)(2,1)S(1)}, bf16[4,256,256]{2,1,0:T(8,128)(2,1)}, u32[]{:S(2)}) %copy-start) | copy-done | bytes 524312
  46.3 13.8 %compress.1 = (bf16[256,256]{1,0:T(8,128)(2,1)S(1)}, bf16[256,256]{1,0:T(8,128)(2,1)}, bf16[256,256]{1,0:T(8,128)(2,1)S(1)}) custom-call(bf16[4,256,256]{2,1,0:T(8,128)(2,1)S(1)} %copy-done, bf16[64,256]{1,0:T(8,128)(2,1)S(1)} %bitcast.8, bf16[256,256]{1,0:T(8,128)(2,1)S(1)} %copy-done.1), custom_call_target="tpu_custom_call" | custom-call | tf_op jit(solution)/shard_map/compress/pallas_call | solution.py:249
  60.1 10.3 %couple.1 = f32[256,1024]{1,0:T(8,128)S(1)} custom-call(bf16[256,256]{1,0:T(8,128)(2,1)S(1)} %get-tuple-element.6.w_ref, bf16[256,256]{1,0:T(8,128)(2,1)S(1)} %get-tuple-element.7.p_ref), custom_call_target="tpu_custom_call" | custom-call | tf_op jit(solution)/shard_map/couple/pallas_call | solution.py:297
  70.4 1.0 %copy.10 = f32[256,1024]{1,0:T(8,128)} copy(f32[256,1024]{1,0:T(8,128)S(1)} %couple.1) | data formatting | bytes 2097152
Async XLA Ops:
  0.6 44.6 %copy-start.1 = (bf16[256,256]{1,0:T(8,128)(2,1)S(1)}, bf16[256,256]{1,0:T(8,128)(2,1)}, u32[]{:S(2)}) copy-start(bf16[256,256]{1,0:T(8,128)(2,1)} %pivot_ref.1) | copy-start | bytes 393220
  0.6 44.6 %copy-start.2 = (bf16[256,64]{0,1:T(8,128)(2,1)S(1)}, bf16[256,64]{0,1:T(8,128)(2,1)}, u32[]{:S(2)}) copy-start(bf16[256,64]{0,1:T(8,128)(2,1)} %param.12) | copy-start | bytes 98308
  45.3 1.0 %copy-start = (bf16[4,256,256]{2,1,0:T(8,128)(2,1)S(1)}, bf16[4,256,256]{2,1,0:T(8,128)(2,1)}, u32[]{:S(2)}) copy-start(bf16[4,256,256]{2,1,0:T(8,128)(2,1)} %merge.1.m_ref) | copy-start | bytes 1572868

commit v3 on v2

--- a/solution.py
+++ b/solution.py
@@ -29,6 +29,16 @@
     return lax.dot_general(
         a, b, (((1,), (0,)), ((), ())), precision=precision, preferred_element_type=F32
     )
+
+
+def works_on_pair(z, chips):
+    return lax.rem(z, 2) == jnp.where(2 * z < chips, 0, 1)
+
+
+def targets_ahead(z, chips):
+    even = lax.rem(z, 2) == 0
+    shift = jnp.where(even, jnp.where(2 * z < chips, -1, 1), 0)
+    return chips - 1 - z + shift
 
 
 def merge_kernel(
@@ -43,6 +53,8 @@
     above = lax.rem(f + 2, 2 * chips)
     below = lax.rem(f + 2 * chips - 2, 2 * chips)
     last = chips - 1
+    up_count = TILES_DEV * targets_ahead(z, chips)
+    dn_count = TILES_DEV * targets_ahead(last - z, chips)
 
     load = pltpu.make_async_copy(pieces_hbm, pieces_ref, load_sem)
     load.start()
@@ -119,7 +131,7 @@
         for s, total in enumerate(partial(2 * t + c)):
             part[t * TILES_DEV + s] = total
 
-        @pl.when(k < last)
+        @pl.when(k < last - 1)
         def _():
             end_flows(k)
 
@@ -129,24 +141,28 @@
         cols = slice(s * R, (s + 1) * R)
         part[z * TILES_DEV + s] += dot_nt(pu_ref[:, cols], pv_ref[:, cols])
 
+    out_ref[...] = jnp.zeros_like(out_ref)
+
     def tick(n, _):
         up_n = n - z
         dn_n = n - (last - z)
 
-        @pl.when((up_n >= 0) & (up_n < TILES_DEV * (last - z)))
+        @pl.when((up_n >= 0) & (up_n < up_count))
         def _():
             flow("up", last - lax.div(up_n, TILES_DEV), lax.rem(up_n, TILES_DEV), True)
 
-        @pl.when((dn_n >= 0) & (dn_n < TILES_DEV * z))
+        @pl.when((dn_n >= 0) & (dn_n < dn_count))
         def _():
             flow("dn", lax.div(dn_n, TILES_DEV), lax.rem(dn_n, TILES_DEV), True)
 
     @pl.when((z > 0) & (z < last))
     def _():
-        lax.fori_loop(0, TILES_DEV * last + last, tick, None)
-
-    def finish(s, _):
-        i = z * TILES_DEV + s
+        lax.fori_loop(0, TILES_DEV * chips + last, tick, None)
+
+    def finish(n, _):
+        place = jnp.where(2 * z < chips, lax.div(n, TILES_DEV), 1 - lax.div(n, TILES_DEV))
+        place = place * TILES_DEV + lax.rem(n, TILES_DEV)
+        i = (z - lax.rem(z, 2)) * TILES_DEV + place
         copy("ex", i).wait_recv()
         part[i] += ex_in[i].astype(F32)
 
@@ -160,18 +176,20 @@
             copy("dn", i).wait_recv()
             part[i] += dn_in[i].astype(F32)
 
-        out_ref[s] = part[i].astype(BF16)
-
-    lax.fori_loop(0, TILES_DEV, finish, None)
+        out_ref[place] = part[i].astype(BF16)
+
+    @pl.when(works_on_pair(z, chips))
+    def _():
+        lax.fori_loop(0, 2 * TILES_DEV, finish, None)
 
     def drain(i, _):
         copy("ex", i).wait_send()
 
-        @pl.when(i >= TILES_DEV * (z + 1))
+        @pl.when(i >= TILES_DEV * chips - up_count)
         def _():
             copy("up", i).wait_send()
 
-        @pl.when(i < TILES_DEV * z)
+        @pl.when(i < dn_count)
         def _():
             copy("dn", i).wait_send()
 
@@ -185,7 +203,7 @@
     tile = (chunks, B, B)
     return pl.pallas_call(
         functools.partial(merge_kernel, chips),
-        out_shape=jax.ShapeDtypeStruct((TILES_DEV, B, B), BF16),
+        out_shape=jax.ShapeDtypeStruct((2 * TILES_DEV, B, B), BF16),
         in_specs=[
             pl.BlockSpec(memory_space=pltpu.SMEM),
             pl.BlockSpec(memory_space=pl.ANY),
@@ -211,7 +229,7 @@
     eye = (
         lax.broadcasted_iota(jnp.int32, (R, R), 0) == lax.broadcasted_iota(jnp.int32, (R, R), 1)
     ).astype(F32)
-    for t in range(TILES_DEV):
+    for t in range(2 * TILES_DEV):
         gram = dot_nt(y[t], y[t], HIGHEST)
         work[:, t, :] = jnp.concatenate((gram, eye), axis=1)
     rows = [work[i] for i in range(R)]
@@ -224,91 +242,131 @@
             rows[i] = rows[i] - row[:, i : i + 1] * scaled
         work[j] = row * inverse
     return [
-        dot_nn(work[:, t, :][:, R:], y[t], HIGHEST).astype(BF16) for t in range(TILES_DEV)
+        dot_nn(work[:, t, :][:, R:], y[t], HIGHEST).astype(BF16) for t in range(2 * TILES_DEV)
     ]
 
 
-def compress_kernel(m_ref, sketch_ref, pivot_ref, w_ref, coeff_ref, pivoted_ref, work):
-    tiles = range(TILES_DEV)
-    work[...] = jnp.ones_like(work)
+def compress_kernel(m_ref, sketch_ref, w_ref, work):
+    tiles = range(2 * TILES_DEV)
     sketch_t = sketch_ref[...]
     y = [dot_nt(sketch_t, m_ref[t]) for t in tiles]
     q = basis(y, work)
     mid = [dot_nn(q[t], m_ref[t]).astype(BF16) for t in tiles]
     y = [dot_nt(mid[t], m_ref[t]) for t in tiles]
     q = basis(y, work)
-    w = jnp.concatenate([dot_nn(q[t], m_ref[t]) for t in tiles], axis=0)
-    w_half = w.astype(BF16)
-    w_ref[...] = w_half
-    pivoted_ref[...] = dot_nt(w_half, pivot_ref[...]).astype(BF16)
-    coeff_ref[...] = w.T.astype(BF16)
-
-
-def compress(merged, sketch, pivot_inverse):
-    wide = TILES_DEV * R
+    for t in tiles:
+        w_ref[t] = dot_nn(q[t], m_ref[t]).astype(BF16)
+
+
+def compress(merged, sketch):
     return pl.pallas_call(
         compress_kernel,
-        out_shape=(
-            jax.ShapeDtypeStruct((wide, B), BF16),
-            jax.ShapeDtypeStruct((B, wide), BF16),
-            jax.ShapeDtypeStruct((wide, B), BF16),
-        ),
-        in_specs=[pl.BlockSpec(memory_space=pltpu.VMEM)] * 3,
-        out_specs=[pl.BlockSpec(memory_space=pltpu.VMEM)] * 3,
-        scratch_shapes=[pltpu.VMEM((R, 8, 2 * R), F32)],
+        out_shape=jax.ShapeDtypeStruct((2 * TILES_DEV, R, B), BF16),
+        in_specs=[pl.BlockSpec(memory_space=pltpu.VMEM)] * 2,
+        out_specs=pl.BlockSpec(memory_space=pltpu.VMEM),
+        scratch_shapes=[pltpu.VMEM((R, 2 * TILES_DEV, 2 * R), F32)],
         compiler_params=pltpu.CompilerParams(vmem_limit_bytes=32 * 2**20),
         name="compress",
-    )(merged, sketch, pivot_inverse)
-
-
-def couple_kernel(ranks, w_ref, p_ref, cores_ref, gathered, send, recv):
+    )(merged, sketch)
+
+
+def couple_kernel(
+    ranks, chips, found_ref, pivot_ref, coeff_ref, cores_ref,
+    w, pivoted, gathered, give_send, give_recv, send, recv,
+):
     me = lax.axis_index("tile")
+    f = lax.axis_index("front")
+    z = lax.div(f, 2)
+    half = lax.rem(z, 2)
+    partner = f + 2 - 4 * half
+    worker = works_on_pair(z, chips)
     barrier = pltpu.get_barrier_semaphore()
+    pl.semaphore_signal(barrier, inc=1, device_id={"front": partner}, device_id_type=MESH)
     for d in range(1, ranks):
         peer = lax.rem(me + d, ranks)
         pl.semaphore_signal(barrier, inc=1, device_id={"tile": peer}, device_id_type=MESH)
-    pl.semaphore_wait(barrier, ranks - 1)
-
-    def copy(d):
+    pl.semaphore_wait(barrier, ranks)
+
+    def give(s):
         return pltpu.make_async_remote_copy(
-            src_ref=p_ref, dst_ref=gathered.at[d - 1], send_sem=send.at[d - 1],
-            recv_sem=recv.at[d - 1], device_id={"tile": lax.rem(me + d, ranks)},
-            device_id_type=MESH,
+            src_ref=found_ref.at[(1 - half) * TILES_DEV + s], dst_ref=w.at[s],
+            send_sem=give_send.at[s], recv_sem=give_recv.at[s],
+            device_id={"front": partner}, device_id_type=MESH,
         )
 
+    def copy(d, s):
+        return pltpu.make_async_remote_copy(
+            src_ref=pivoted.at[s], dst_ref=gathered.at[d - 1, s],
+            send_sem=send.at[d - 1, s], recv_sem=recv.at[d - 1, s],
+            device_id={"tile": lax.rem(me + d, ranks)}, device_id_type=MESH,
+        )
+
+    @pl.when(worker)
+    def _():
+        for s in range(TILES_DEV):
+            give(s).start()
+        for s in range(TILES_DEV):
+            w[s] = found_ref[half * TILES_DEV + s]
+
+    for s in range(TILES_DEV):
+        @pl.when(jnp.logical_not(worker))
+        def _():
+            give(s).wait_recv()
+
+        pivoted[s] = dot_nt(w[s], pivot_ref[...]).astype(BF16)
+        for d in range(1, ranks):
+            copy(d, s).start()
+
+    wide = TILES_DEV * R
+    own = w[...].reshape(wide, B)
+
+    def place(source, block):
+        cores_ref[:, pl.ds(pl.multiple_of(source * wide, wide), wide)] = dot_nt(
+            own, block.reshape(wide, B)
+        )
+
+    place(me, pivoted[...])
+    coeff_ref[...] = own.astype(F32).T.astype(BF16)
     for d in range(1, ranks):
-        copy(d).start()
-    wide = TILES_DEV * R
-
-    def place(source, block):
-        cores_ref[:, pl.ds(pl.multiple_of(source * wide, wide), wide)] = dot_nt(w_ref[...], block)
-
-    place(me, p_ref[...])
-    for d in range(1, ranks):
-        copy(d).wait_recv()
+        for s in range(TILES_DEV):
+            copy(d, s).wait_recv()
         place(lax.rem(me + ranks - d, ranks), gathered[d - 1])
     for d in range(1, ranks):
-        copy(d).wait_send()
-
-
-def couple(w, pivoted):
+        for s in range(TILES_DEV):
+            copy(d, s).wait_send()
+
+    @pl.when(worker)
+    def _():
+        for s in range(TILES_DEV):
+            give(s).wait_send()
+
+
+def couple(found, pivot_inverse):
     ranks = lax.axis_size("tile")
+    chips = lax.axis_size("front") // 2
     wide = TILES_DEV * R
     return pl.pallas_call(
-        functools.partial(couple_kernel, ranks),
-        out_shape=jax.ShapeDtypeStruct((wide, ranks * wide), F32),
+        functools.partial(couple_kernel, ranks, chips),
+        out_shape=(
+            jax.ShapeDtypeStruct((B, wide), BF16),
+            jax.ShapeDtypeStruct((wide, ranks * wide), F32),
+        ),
         in_specs=[pl.BlockSpec(memory_space=pltpu.VMEM)] * 2,
-        out_specs=pl.BlockSpec(memory_space=pltpu.VMEM),
+        out_specs=[pl.BlockSpec(memory_space=pltpu.VMEM)] * 2,
         scratch_shapes=[
-            pltpu.VMEM((ranks - 1, wide, B), BF16),
-            pltpu.SemaphoreType.DMA((ranks - 1,)),
-            pltpu.SemaphoreType.DMA((ranks - 1,)),
+            pltpu.VMEM((TILES_DEV, R, B), BF16),
+            pltpu.VMEM((TILES_DEV, R, B), BF16),
+            pltpu.VMEM((ranks - 1, TILES_DEV, R, B), BF16),
+            pltpu.SemaphoreType.DMA((TILES_DEV,)),
+            pltpu.SemaphoreType.DMA((TILES_DEV,)),
+            pltpu.SemaphoreType.DMA((ranks - 1, TILES_DEV)),
+            pltpu.SemaphoreType.DMA((ranks - 1, TILES_DEV)),
         ],
         compiler_params=pltpu.CompilerParams(
             collective_id=1, has_side_effects=True, vmem_limit_bytes=32 * 2**20
         ),
         name="couple",
-    )(w, pivoted)
+    )(found, pivot_inverse)
 
 
 def shards(pieces, dest_front, dest_slot, parent_u, parent_v, sketch, pivot_inverse):
@@ -327,8 +385,7 @@
     code = (ids * 8 + dest_slot - TILES_DEV)[:, None]
     table = jnp.sum(jnp.where(hit, code, 0), axis=0) + TILES_DEV
     merged = merge(table, pieces, parent_u, parent_v)
-    w, coeff, pivoted = compress(merged, sketch.T, pivot_inverse)
-    return (coeff, couple(w, pivoted))
+    return couple(compress(merged, sketch.T), pivot_inverse)
 
 
 def solution(mesh):

time: 72.5 us -> 75.6 us (1.043)
  Pallas kernels: 65.8 us -> 68.1 us
  local copies, waits for them, and re-layouts: 2.02 us -> 2.85 us
    pallas_call x1, Pallas kernels: 41.7 us -> 45.5 us  [merge(): pl.pallas_call(functools.partial(merge_kernel, chips), out_shape=jax.Shap...]
    pallas_call x2, Pallas kernels: 24.1 us -> 22.6 us  [the longest x1 14.3 us: compress(): pl.pallas_call(compress_kernel, out_shape=jax.ShapeDtypeStruct((2 * TILES...]
    unnamed x7 -> x8, local copies, waits for them, and re-layouts: 2.02 us -> 2.85 us
where the time goes in v3:
time: 75.6 us; the launch traced here: 74.5 us
  Pallas kernels  68.1 us (90%)
  other arithmetic  2.9 us (4%)
  local copies, waits for them, and re-layouts  2.85 us (4%)
    pallas_call x1, Pallas kernels, merge(): pl.pallas_call(functools.partial(merge_kernel, chips), out_shape=jax.Shap...  45.5 us
    pallas_call x1, Pallas kernels, compress(): pl.pallas_call(compress_kernel, out_shape=jax.ShapeDtypeStruct((2 * TILES...  14.3 us
    pallas_call x1, Pallas kernels, couple(): pl.pallas_call(functools.partial(couple_kernel, ranks, chips), out_shape=...  8.26 us
    unnamed x8, local copies, waits for them, and re-layouts  2.85 us

profile of v3, /device:TPU:0, one launch (start us, length us, event | category | flops | bytes accessed | tf_op | source)
XLA Modules:
  0.0 74.5 jit_solution(1172457282238121724)
XLA Ops:
  0.6 0.0 copy-start.1
  0.6 0.0 copy-start.2
  0.7 0.7 add_add_fusion
  1.4 0.9 %convert_reduce_fusion = s32[72]{0:T(128)S(1)} fusion(s32[72]{0:T(128)} %bitcast.9), kind=kLoop, calls=%fused_computation.2 | loop fusion | flops 25848 | bytes 576 | tf_op jit(solution)/shard_map/reduce_sum | solution.py:377
  2.3 0.7 fusion.1
  2.9 0.1 select_reduce_fusion
  3.0 0.5 broadcast_add_fusion.table_ref
  3.6 45.5 %merge.1.m_ref = bf16[8,256,256]{2,1,0:T(8,128)(2,1)} custom-call(s32[80]{0:T(128)} %broadcast_add_fusion.table_ref, bf16[72,256,128]{2,1,0:T(8,128)(2,1)} %pieces_hbm.1, bf16[256,256]{1,0:T(8,128)(2,1)} %pu_ref.1, bf16[256,256]{1,0:T(8,128)(2,1)} %pv_ref.1), custom_call_target="tpu_custom_call" | custom-call | tf_op jit(solution)/shard_map/merge/pallas_call | solution.py:204
  49.1 0.0 copy-done.2
  49.1 0.0 copy-start
  49.1 1.2 %copy-done = bf16[8,256,256]{2,1,0:T(8,128)(2,1)S(1)} copy-done((bf16[8,256,256]{2,1,0:T(8,128)(2,1)S(1)}, bf16[8,256,256]{2,1,0:T(8,128)(2,1)}, u32[]{:S(2)}) %copy-start) | copy-done | bytes 1048600
  50.3 14.3 %compress.1.found_ref = bf16[8,64,256]{2,1,0:T(8,128)(2,1)S(1)} custom-call(bf16[8,256,256]{2,1,0:T(8,128)(2,1)S(1)} %copy-done, bf16[64,256]{1,0:T(8,128)(2,1)S(1)} %bitcast.8), custom_call_target="tpu_custom_call" | custom-call | tf_op jit(solution)/shard_map/compress/pallas_call | solution.py:262
  64.6 0.0 copy-done.1
  64.6 8.3 %couple.1 = (bf16[256,256]{1,0:T(8,128)(2,1)S(1)}, f32[256,1024]{1,0:T(8,128)S(1)}) custom-call(bf16[8,64,256]{2,1,0:T(8,128)(2,1)S(1)} %compress.1.found_ref, bf16[256,256]{1,0:T(8,128)(2,1)S(1)} %copy-done.1), custom_call_target="tpu_custom_call" | custom-call | tf_op jit(solution)/shard_map/couple/pallas_call | solution.py:348
  72.9 0.7 copy.11
  73.5 1.0 %copy.12 = f32[256,1024]{1,0:T(8,128)} copy(f32[256,1024]{1,0:T(8,128)S(1)} %get-tuple-element.5) | data formatting | bytes 2097152
Async XLA Ops:
  0.6 64.0 %copy-start.1 = (bf16[256,256]{1,0:T(8,128)(2,1)S(1)}, bf16[256,256]{1,0:T(8,128)(2,1)}, u32[]{:S(2)}) copy-start(bf16[256,256]{1,0:T(8,128)(2,1)} %pivot_ref.1) | copy-start | bytes 393220
  0.6 48.4 %copy-start.2 = (bf16[256,64]{0,1:T(8,128)(2,1)S(1)}, bf16[256,64]{0,1:T(8,128)(2,1)}, u32[]{:S(2)}) copy-start(bf16[256,64]{0,1:T(8,128)(2,1)} %param.12) | copy-start | bytes 98308
  49.1 1.2 %copy-start = (bf16[8,256,256]{2,1,0:T(8,128)(2,1)S(1)}, bf16[8,256,256]{2,1,0:T(8,128)(2,1)}, u32[]{:S(2)}) copy-start(bf16[8,256,256]{2,1,0:T(8,128)(2,1)} %merge.1.m_ref) | copy-start | bytes 3145732

commit v4 on v2

--- a/solution.py
+++ b/solution.py
@@ -87,9 +87,11 @@
         left = jnp.concatenate(lefts, axis=1)
         right = jnp.concatenate(rights, axis=1)
         owner = jnp.concatenate(owners, axis=1)
-        for s in range(TILES_DEV):
-            mask = jnp.where(owner == s, 1.0, 0.0).astype(BF16)
-            yield dot_nt(left * mask, right)
+        masked = [
+            left * jnp.where(owner == s, 1.0, 0.0).astype(BF16) for s in range(TILES_DEV)
+        ]
+        product = dot_nt(jnp.concatenate(masked, axis=0), right)
+        return [product[s * B : (s + 1) * B] for s in range(TILES_DEV)]
 
     def flow(kind, t, s, incoming):
         i = t * TILES_DEV + s

time: 72.5 us -> 72.5 us (level)
  no operation moved by 1% of the time
where the time goes in v4:
time: 72.5 us; the launch traced here: 71.4 us
  Pallas kernels  65.8 us (91%)
  other arithmetic  2.89 us (4%)
  local copies, waits for them, and re-layouts  2.02 us (3%)
    pallas_call x1, Pallas kernels, merge(): pl.pallas_call(functools.partial(merge_kernel, chips), out_shape=jax.Shap...  42.1 us
    pallas_call x1, Pallas kernels, compress(): pl.pallas_call(compress_kernel, out_shape=(jax.ShapeDtypeStruct((wide, B)...  13.8 us
    pallas_call x1, Pallas kernels, couple(): pl.pallas_call(functools.partial(couple_kernel, ranks), out_shape=jax.Sha...  10 us
    unnamed x7, local copies, waits for them, and re-layouts  2.02 us

profile of v4, /device:TPU:0, one launch (start us, length us, event | category | flops | bytes accessed | tf_op | source)
XLA Modules:
  0.0 71.4 jit_solution(8755158233516458282)
XLA Ops:
  0.6 0.0 copy-start.1
  0.6 0.0 copy-start.2
  0.7 0.7 add_add_fusion
  1.3 0.9 %convert_reduce_fusion = s32[72]{0:T(128)S(1)} fusion(s32[72]{0:T(128)} %bitcast.9), kind=kLoop, calls=%fused_computation.2 | loop fusion | flops 25848 | bytes 576 | tf_op jit(solution)/shard_map/reduce_sum | solution.py:321
  2.3 0.7 fusion.1
  2.9 0.1 select_reduce_fusion
  3.0 0.5 broadcast_add_fusion.table_ref
  3.5 42.1 %merge.1.m_ref = bf16[4,256,256]{2,1,0:T(8,128)(2,1)} custom-call(s32[80]{0:T(128)} %broadcast_add_fusion.table_ref, bf16[72,256,128]{2,1,0:T(8,128)(2,1)} %pieces_hbm.1, bf16[256,256]{1,0:T(8,128)(2,1)} %pu_ref.1, bf16[256,256]{1,0:T(8,128)(2,1)} %pv_ref.1), custom_call_target="tpu_custom_call" | custom-call | tf_op jit(solution)/shard_map/merge/pallas_call | solution.py:188
  45.6 0.0 copy-done.1
  45.6 0.0 copy-done.2
  45.6 0.0 copy-start
  45.6 1.0 %copy-done = bf16[4,256,256]{2,1,0:T(8,128)(2,1)S(1)} copy-done((bf16[4,256,256]{2,1,0:T(8,128)(2,1)S(1)}, bf16[4,256,256]{2,1,0:T(8,128)(2,1)}, u32[]{:S(2)}) %copy-start) | copy-done | bytes 524312
  46.7 13.8 %compress.1 = (bf16[256,256]{1,0:T(8,128)(2,1)S(1)}, bf16[256,256]{1,0:T(8,128)(2,1)}, bf16[256,256]{1,0:T(8,128)(2,1)S(1)}) custom-call(bf16[4,256,256]{2,1,0:T(8,128)(2,1)S(1)} %copy-done, bf16[64,256]{1,0:T(8,128)(2,1)S(1)} %bitcast.8, bf16[256,256]{1,0:T(8,128)(2,1)S(1)} %copy-done.1), custom_call_target="tpu_custom_call" | custom-call | tf_op jit(solution)/shard_map/compress/pallas_call | solution.py:251
  60.4 10.0 %couple.1 = f32[256,1024]{1,0:T(8,128)S(1)} custom-call(bf16[256,256]{1,0:T(8,128)(2,1)S(1)} %get-tuple-element.6.w_ref, bf16[256,256]{1,0:T(8,128)(2,1)S(1)} %get-tuple-element.7.p_ref), custom_call_target="tpu_custom_call" | custom-call | tf_op jit(solution)/shard_map/couple/pallas_call | solution.py:299
  70.4 1.0 %copy.10 = f32[256,1024]{1,0:T(8,128)} copy(f32[256,1024]{1,0:T(8,128)S(1)} %couple.1) | data formatting | bytes 2097152
Async XLA Ops:
  0.6 45.0 %copy-start.1 = (bf16[256,256]{1,0:T(8,128)(2,1)S(1)}, bf16[256,256]{1,0:T(8,128)(2,1)}, u32[]{:S(2)}) copy-start(bf16[256,256]{1,0:T(8,128)(2,1)} %pivot_ref.1) | copy-start | bytes 393220
  0.6 45.0 %copy-start.2 = (bf16[256,64]{0,1:T(8,128)(2,1)S(1)}, bf16[256,64]{0,1:T(8,128)(2,1)}, u32[]{:S(2)}) copy-start(bf16[256,64]{0,1:T(8,128)(2,1)} %param.12) | copy-start | bytes 98308
  45.6 1.0 %copy-start = (bf16[4,256,256]{2,1,0:T(8,128)(2,1)S(1)}, bf16[4,256,256]{2,1,0:T(8,128)(2,1)}, u32[]{:S(2)}) copy-start(bf16[4,256,256]{2,1,0:T(8,128)(2,1)} %merge.1.m_ref) | copy-start | bytes 1572868
